TPU v7x, 32 devices: a whole 2x2x4 slice. The times are simulated.
32 devices in a mesh: row: 4 (over z), col: 8 (over y, x, core).
Axes of the slice: x: 2, y: 2, z: 4, core: 2. Of those that a mesh axis runs over, the one named last changes fastest.
Arguments:
- right_side: float32 [4096, 4, 128], P(('row', 'col')), may hold values from -60 to 60
- cluster_of: int32 [4096], P(('row', 'col')), may hold values from 0 to 4095, as said below
- near_rows: int32 [12288], P(('row', 'col')), may hold values from 0 to 127
- near_columns: int32 [12288], P(('row', 'col')), may hold values from 0 to 191, as said below
- near_blocks: bfloat16 [12288, 128, 128], P(('row', 'col')), may hold values from -1 to 1
- far_rows: int32 [32768], P(('row', 'col')), may hold values from 0 to 1023, as said below
- far_columns: int32 [32768], P(('row', 'col')), may hold values from 0 to 511
- far_rank: int32 [32768], P(('row', 'col')), may hold values from 4 to 16
- far_left: bfloat16 [32768, 16, 128], P(('row', 'col')), may hold values from -1.5 to 1.5
- far_right: bfloat16 [32768, 16, 128], P(('row', 'col')), may hold values from -0.5 to 0.5
Outputs:
- second_basis: float32 [4096, 4, 128], P(('row', 'col'))
- next_vector: float32 [4096, 4, 128], P(('row', 'col'))
- hessenberg: float32 [5, 4], replicated
Inputs may be any that keep to these rules, and one draw needn't show every extreme that they name: `cluster_of`: A permutation of the cluster positions; position g belongs to the device of index g // 128 along row+col. Each device's blocks go to at most 8 blocks a destination device, and exactly 8 to some. `near_columns`: position 32 is the device's own first block; entries never point before the first or after the last block of cluster order. `far_rows`: in each device's list, the k-th group of 128 entries has rows in blocks k * 128 to (k + 1) * 128 - 1 of the row cluster.
All inputs are finite; a program needn't handle non-finite values.
Results may differ from a plain program's by a relative error of at most 0.0018.
The roundings to bfloat16 on the way count: a program that leaves them out, or rounds other values in their place, can miss the bound.
Values may be sent and summed in bfloat16 or wider, within the bound.
A program may use at most 128 MiB of HBM per device.

v0:
```python
import jax
import jax.numpy as jnp
from jax import lax
from jax.sharding import PartitionSpec as P

epsilon = 1e-06


def padded(cells, sides, width):
    for axis, dim in sides:
        count = lax.axis_size(axis)
        ends = count - 1
        head = lax.slice_in_dim(cells, 0, width, axis=dim)
        tail = lax.slice_in_dim(cells, cells.shape[dim] - width, cells.shape[dim], axis=dim)
        cells = jnp.concatenate(
            [
                lax.ppermute(tail, axis, [(i, (i + 1) % count) for i in range(ends)]),
                cells,
                lax.ppermute(head, axis, [((i + 1) % count, i) for i in range(ends)]),
            ],
            axis=dim,
        )
    return cells


def body(
    right_side,
    cluster_of,
    near_rows,
    near_columns,
    near_blocks,
    far_rows,
    far_columns,
    far_rank,
    far_left,
    far_right,
):
    row_count = lax.axis_size("row")
    column_count = lax.axis_size("col")
    device_count = row_count * column_count
    local_blocks = right_side.shape[0]
    sides = right_side.shape[1]
    width = right_side.shape[2]
    capacity = 2 * local_blocks // device_count
    halo_width = local_blocks // 4
    panels = local_blocks * device_count * width
    max_rank = far_left.shape[1]
    target = cluster_of // local_blocks
    place = cluster_of % local_blocks
    order = jnp.arange(local_blocks, dtype=jnp.int32)
    earlier = (target[None, :] == target[:, None]) & (order[None, :] < order[:, None])
    slot_index = jnp.sum(earlier.astype(jnp.int32), axis=1)
    position_send = (
        jnp.full((device_count, capacity), local_blocks, jnp.int32)
        .at[target, slot_index]
        .set(place)
    )
    position_recv = lax.all_to_all(
        position_send, ("row", "col"), split_axis=0, concat_axis=0, tiled=True
    ).reshape(-1)
    fetch_index = jnp.minimum(position_recv, local_blocks - 1)
    rank_mask = (jnp.arange(max_rank, dtype=jnp.int32)[None, :] < far_rank[:, None]).astype(
        jnp.float32
    )[:, :, None]

    def relay_in(vector):
        rounded = vector.astype(jnp.bfloat16)
        outgoing = (
            jnp.zeros((device_count, capacity, sides, width), jnp.bfloat16)
            .at[target, slot_index]
            .set(rounded)
        )
        arrived = lax.all_to_all(outgoing, ("row", "col"), split_axis=0, concat_axis=0, tiled=True)
        arrived = arrived.reshape(device_count * capacity, sides, width)
        return (
            jnp.zeros((local_blocks, sides, width), jnp.bfloat16)
            .at[position_recv]
            .set(arrived, mode="drop")
        )

    def relay_out(image_sum):
        outgoing = image_sum[fetch_index].reshape(device_count, capacity, sides, width)
        returned = lax.all_to_all(outgoing, ("row", "col"), split_axis=0, concat_axis=0, tiled=True)
        return returned[target, slot_index]

    def apply_clustered(clustered):
        extended = padded(clustered, ((("row", "col"), 0),), halo_width)
        near_out = jnp.einsum(
            "ekp,eqp->eqk", near_blocks, extended[near_columns], preferred_element_type=jnp.float32
        )
        image_sum = 0.5 * clustered.astype(jnp.float32)
        image_sum = image_sum.at[near_rows].add(near_out)
        gathered = lax.all_gather(clustered, "row", axis=0, tiled=True)
        coefficients = jnp.einsum(
            "etp,eqp->etq", far_right, gathered[far_columns], preferred_element_type=jnp.float32
        )
        coefficients = (coefficients * rank_mask).astype(jnp.bfloat16)
        far_out = jnp.einsum(
            "etq,etk->eqk", coefficients, far_left, preferred_element_type=jnp.float32
        )
        partial_value = (
            jnp.zeros((local_blocks * column_count, sides, width), jnp.float32)
            .at[far_rows]
            .add(far_out)
        )
        image_sum = image_sum + lax.psum_scatter(
            partial_value, "col", scatter_dimension=0, tiled=True
        )
        return image_sum

    def operate_mesh(vector):
        return relay_out(apply_clustered(relay_in(vector)))

    def local_inner(left_vector, right_vector):
        return jnp.sum(left_vector * right_vector, axis=(0, 2))

    side_norm = jnp.sqrt(
        lax.psum(local_inner(right_side, right_side), ("row", "col")) / panels + epsilon
    )
    first = right_side / side_norm[None, :, None]
    image_one = operate_mesh(first)
    project_one = lax.psum(local_inner(first, image_one), ("row", "col")) / panels
    remainder = image_one - project_one[None, :, None] * first
    norm_two = jnp.sqrt(
        lax.psum(local_inner(remainder, remainder), ("row", "col")) / panels + epsilon
    )
    second_basis = remainder / norm_two[None, :, None]
    image_two = operate_mesh(second_basis)
    sum_two, sum_three = lax.psum(
        (local_inner(first, image_two), local_inner(second_basis, image_two)), ("row", "col")
    )
    project_two = sum_two / panels
    project_three = sum_three / panels
    next_vector = (
        image_two - project_two[None, :, None] * first - project_three[None, :, None] * second_basis
    )
    second_basis, next_vector, entries = (
        second_basis,
        next_vector,
        (project_one, norm_two, project_two, project_three),
    )
    project_one, norm_two, project_two, project_three = entries
    hessenberg = jnp.stack([side_norm, project_one, norm_two, project_two, project_three])
    return (second_basis, next_vector, hessenberg)


def solution(mesh):
    placed = (
        P(("row", "col"), None, None),
        P(("row", "col")),
        P(("row", "col")),
        P(("row", "col")),
        P(("row", "col"), None, None),
        P(("row", "col")),
        P(("row", "col")),
        P(("row", "col")),
        P(("row", "col"), None, None),
        P(("row", "col"), None, None),
    )
    return jax.shard_map(
        body,
        mesh=mesh,
        in_specs=placed,
        out_specs=(P(("row", "col"), None, None), P(("row", "col"), None, None), P()),
        check_vma=False,
    )
```

profile of v0, /device:TPU:0, one launch (start us, length us, event | category | flops | bytes accessed | tf_op | source)
XLA Modules:
  0.0 642.0 jit_solution(10303565593195334214)
XLA Ops:
  15.2 7.3 %all-to-all-start = ((s32[32,1,8]{2,1,0:T(1,128)}), s32[32,1,8]{2,1,0:T(1,128)S(1)}, u32[]{:S(2)}, u32[]{:S(2)}) async-start(s32[32,1,8]{2,1,0:T(1,128)} %copy.18), calls=%async_computation | async-start | bytes 32768 | tf_op jit(solution)/shard_map/all_to_all | solution.py:58
  24.4 40.5 %psum.35 = f32[4]{0:T(128)S(1)} all-reduce(f32[4]{0:T(128)S(1)} %multiply_reduce_fusion.4), channel_id=1, replica_groups=mesh['row'=4,'col'=8] {'row','col'}, use_global_device_ids=true, to_apply=%region_3.4 | all-reduce | flops 4 | bytes 32 | tf_op jit(solution)/shard_map/psum | solution.py:118
  66.8 14.8 %scatter_fusion.1 = bf16[32,8,4,128]{3,2,1,0:T(4,128)(2,1)} fusion(bf16[32,8,4,128]{3,2,1,0:T(4,128)(2,1)} %broadcast.143.clone, s32[128]{0:T(128)S(1)} %get-tuple-element.28, bf16[128,4,128]{2,1,0:T(4,128)(2,1)S(1)} %get-tuple-element.21), kind=kCustom, calls=%fused_computation.9 | custom fusion | bytes 394240 | tf_op jit(solution)/shard_map/scatter | solution.py:71
  88.9 7.8 %all-to-all-done.1 = bf16[32,8,4,128]{3,2,1,0:T(4,128)(2,1)S(1)} async-done(((bf16[32,8,4,128]{3,2,1,0:T(4,128)(2,1)}), bf16[32,8,4,128]{3,2,1,0:T(4,128)(2,1)S(1)}, u32[]{:S(2)}, u32[]{:S(2)}) %all-to-all-start.1) | async-done | bytes 262176 | tf_op jit(solution)/shard_map/all_to_all | solution.py:73
  96.7 7.3 %scatter_fusion.2 = bf16[128,4,128]{2,1,0:T(4,128)(2,1)S(1)} fusion(bf16[128,4,128]{2,1,0:T(4,128)(2,1)S(1)} %broadcast.137.clone, s32[256]{0:T(256)S(1)} %bitcast.57, bf16[256,4,128]{2,1,0:T(4,128)(2,1)S(1)} %bitcast.55), kind=kCustom, calls=%fused_computation.10 | custom fusion | bytes 787456 | tf_op jit(solution)/shard_map/scatter | solution.py:78
  104.1 15.9 %all_gather.6 = bf16[512,4,128]{2,1,0:T(4,128)(2,1)S(1)} all-gather(bf16[128,4,128]{2,1,0:T(4,128)(2,1)S(1)} %scatter_fusion.2), channel_id=1, replica_groups=mesh['row'=4,'col'=8] {'row'}, dimensions={0}, use_global_device_ids=true | all-gather | bytes 655360 | tf_op jit(solution)/shard_map/all_gather | solution.py:93
  123.5 8.3 %fusion = f32[1024,4,128]{2,1,0:T(4,128)} fusion(bf16[1024,16,128]{2,1,0:T(8,128)(2,1)} %param.18, bf16[1024,4,128]{2,1,0:T(4,128)(2,1)S(1)} %gather_fusion, bf16[1024,16,128]{2,1,0:T(8,128)(2,1)} %param.19, f32[1024,16]{1,0:T(8,128)S(1)} %fusion.4), kind=kOutput, calls=%fused_computation.19 | convolution fusion | flops 33685504 | bytes 11599872 | tf_op jit(solution)/shard_map/etq,etk->eqk/dot_general | solution.py:98
  132.1 66.4 %scatter_fusion.3 = f32[1024,4,128]{2,1,0:T(4,128)S(1)} fusion(f32[1024,4,128]{2,1,0:T(4,128)S(1)} %broadcast.147.clone, s32[1024]{0:T(1024)S(1)} %compare_select_fusion.1, f32[1024,4,128]{2,1,0:T(4,128)} %fusion), kind=kCustom, calls=%fused_computation.11 | custom fusion | flops 524288 | bytes 6295552 | tf_op jit(solution)/shard_map/scatter-add | solution.py:104
  207.3 9.6 %fusion.20 = f32[384,4,128]{2,1,0:T(4,128)S(1)} fusion(bf16[384,4,128]{2,1,0:T(4,128)(2,1)S(1)} %gather_fusion.1, bf16[384,128,128]{2,1,0:T(8,128)(2,1)} %param.14), kind=kOutput, calls=%fused_computation.78 | convolution fusion | flops 50331648 | bytes 13762560 | tf_op jit(solution)/shard_map/ekp,eqp->eqk/dot_general | solution.py:88
  216.9 42.0 %all-reduce.6.cloned.1.call-done = f32[1024,4,128]{2,1,0:T(4,128)} async-done(((f32[1024,4,128]{2,1,0:T(4,128)}), f32[1024,4,128]{2,1,0:T(4,128)}) %all-reduce.6.cloned.1.call-update) | async-done | bytes 2097168
  260.0 14.2 %scatter_fusion.4 = f32[128,4,128]{2,1,0:T(4,128)S(1)} fusion(f32[128,4,128]{2,1,0:T(4,128)S(1)} %dynamic-slice_add_fusion.1, s32[384]{0:T(512)S(1)} %compare_select_fusion.5, f32[384,4,128]{2,1,0:T(4,128)S(1)} %fusion.20), kind=kCustom, calls=%fused_computation.12 | custom fusion | flops 196608 | bytes 2360832 | tf_op jit(solution)/shard_map/scatter-add | solution.py:92
  275.2 19.2 %all_to_all.29 = f32[32,8,4,128]{3,2,1,0:T(4,128)S(1)} all-to-all(f32[32,8,4,128]{3,2,1,0:T(4,128)S(1)} %bitcast.54), channel_id=1, replica_groups=mesh['row'=4,'col'=8] {'row','col'}, dimensions={0} | all-to-all | bytes 1048576 | tf_op jit(solution)/shard_map/all_to_all | solution.py:83
  295.6 39.0 %psum.36 = f32[4]{0:T(128)S(1)} all-reduce(f32[4]{0:T(128)S(1)} %multiply_reduce_fusion.3), channel_id=1, replica_groups=mesh['row'=4,'col'=8] {'row','col'}, use_global_device_ids=true, to_apply=%region_10.11 | all-reduce | flops 4 | bytes 32 | tf_op jit(solution)/shard_map/psum | solution.py:122
  334.9 40.0 %psum.37 = f32[4]{0:T(128)S(1)} all-reduce(f32[4]{0:T(128)S(1)} %multiply_reduce_fusion.2), channel_id=1, replica_groups=mesh['row'=4,'col'=8] {'row','col'}, use_global_device_ids=true, to_apply=%region_12.13 | all-reduce | flops 4 | bytes 32 | tf_op jit(solution)/shard_map/psum | solution.py:125
  380.9 14.6 %all_to_all.30 = bf16[32,8,4,128]{3,2,1,0:T(4,128)(2,1)S(1)} all-to-all(bf16[32,8,4,128]{3,2,1,0:T(4,128)(2,1)S(1)} %scatter_fusion.5), channel_id=1, replica_groups=mesh['row'=4,'col'=8] {'row','col'}, dimensions={0} | all-to-all | bytes 524288 | tf_op jit(solution)/shard_map/all_to_all | solution.py:73
  395.6 7.3 %scatter_fusion.6 = bf16[128,4,128]{2,1,0:T(4,128)(2,1)S(1)} fusion(bf16[128,4,128]{2,1,0:T(4,128)(2,1)S(1)} %broadcast.137, s32[256]{0:T(256)S(1)} %bitcast.58, bf16[256,4,128]{2,1,0:T(4,128)(2,1)S(1)} %bitcast.56), kind=kCustom, calls=%fused_computation.14 | custom fusion | bytes 787456 | tf_op jit(solution)/shard_map/scatter | solution.py:78
  402.9 15.9 %all_gather.7 = bf16[512,4,128]{2,1,0:T(4,128)(2,1)S(1)} all-gather(bf16[128,4,128]{2,1,0:T(4,128)(2,1)S(1)} %scatter_fusion.6), channel_id=1, replica_groups=mesh['row'=4,'col'=8] {'row'}, dimensions={0}, use_global_device_ids=true | all-gather | bytes 655360 | tf_op jit(solution)/shard_map/all_gather | solution.py:93
  422.4 8.3 %fusion.1 = f32[1024,4,128]{2,1,0:T(4,128)} fusion(bf16[1024,16,128]{2,1,0:T(8,128)(2,1)} %param.18, bf16[1024,4,128]{2,1,0:T(4,128)(2,1)S(1)} %gather_fusion.4, bf16[1024,16,128]{2,1,0:T(8,128)(2,1)} %param.19, f32[1024,16]{1,0:T(8,128)S(1)} %fusion.4), kind=kOutput, calls=%fused_computation.20 | convolution fusion | flops 33685504 | bytes 11599872 | tf_op jit(solution)/shard_map/etq,etk->eqk/dot_general | solution.py:98
  431.0 66.4 %scatter_fusion.7 = f32[1024,4,128]{2,1,0:T(4,128)S(1)} fusion(f32[1024,4,128]{2,1,0:T(4,128)S(1)} %broadcast.147, s32[1024]{0:T(1024)S(1)} %compare_select_fusion.1, f32[1024,4,128]{2,1,0:T(4,128)} %fusion.1), kind=kCustom, calls=%fused_computation.15 | custom fusion | flops 524288 | bytes 6295552 | tf_op jit(solution)/shard_map/scatter-add | solution.py:104
  506.1 9.6 %fusion.21 = f32[384,4,128]{2,1,0:T(4,128)S(1)} fusion(bf16[384,4,128]{2,1,0:T(4,128)(2,1)S(1)} %gather_fusion.5, bf16[384,128,128]{2,1,0:T(8,128)(2,1)} %param.14), kind=kOutput, calls=%fused_computation.79 | convolution fusion | flops 50331648 | bytes 13762560 | tf_op jit(solution)/shard_map/ekp,eqp->eqk/dot_general | solution.py:88
  515.7 42.1 %all-reduce.8.cloned.1.call-done = f32[1024,4,128]{2,1,0:T(4,128)} async-done(((f32[1024,4,128]{2,1,0:T(4,128)}), f32[1024,4,128]{2,1,0:T(4,128)}) %all-reduce.8.cloned.1.call-update) | async-done | bytes 2097168
  558.9 14.2 %scatter_fusion.8 = f32[128,4,128]{2,1,0:T(4,128)S(1)} fusion(f32[128,4,128]{2,1,0:T(4,128)S(1)} %dynamic-slice_add_fusion, s32[384]{0:T(512)S(1)} %compare_select_fusion.5, f32[384,4,128]{2,1,0:T(4,128)S(1)} %fusion.21), kind=kCustom, calls=%fused_computation.16 | custom fusion | flops 196608 | bytes 2360832 | tf_op jit(solution)/shard_map/scatter-add | solution.py:92
  574.1 19.2 %all_to_all.31 = f32[32,8,4,128]{3,2,1,0:T(4,128)S(1)} all-to-all(f32[32,8,4,128]{3,2,1,0:T(4,128)S(1)} %bitcast.53), channel_id=1, replica_groups=mesh['row'=4,'col'=8] {'row','col'}, dimensions={0} | all-to-all | bytes 1048576 | tf_op jit(solution)/shard_map/all_to_all | solution.py:83
  594.6 39.0 %all-reduce.2 = (f32[4]{0:T(128)S(1)}, f32[4]{0:T(128)S(1)}) all-reduce(f32[4]{0:T(128)S(1)} %get-tuple-element.16, f32[4]{0:T(128)S(1)} %get-tuple-element.15), channel_id=1, replica_groups=mesh['row'=4,'col'=8] {'row','col'}, use_global_device_ids=true, to_apply=%region_21.22 | all-reduce | flops 8 | bytes 64 | tf_op jit(solution)/shard_map/psum | solution.py:129
  (82 shorter events, 57.9 us)
Async XLA Ops:
  7.2 79.0 %copy-start.7 = (u32[32]{0:T(128)S(1)}, u32[32]{0:T(128)}, u32[]{:S(2)}) copy-start(u32[32]{0:T(128)} %constant.140) | copy-start | bytes 388
  7.2 58.8 %copy-start.4 = (s32[1024]{0:T(1024)S(1)}, s32[1024]{0:T(1024)}, u32[]{:S(2)}) copy-start(s32[1024]{0:T(1024)} %param.16) | copy-start | bytes 12292
  7.2 58.8 %copy-start.5 = (s32[384]{0:T(512)S(1)}, s32[384]{0:T(512)}, u32[]{:S(2)}) copy-start(s32[384]{0:T(512)} %param.12) | copy-start | bytes 4612
  7.2 58.8 %copy-start.6 = (s32[384]{0:T(512)S(1)}, s32[384]{0:T(512)}, u32[]{:S(2)}) copy-start(s32[384]{0:T(512)} %param.13) | copy-start | bytes 4612
  7.2 80.2 %copy-start.3 = (s32[1024]{0:T(1024)S(1)}, s32[1024]{0:T(1024)}, u32[]{:S(2)}) copy-start(s32[1024]{0:T(1024)} %param.17) | copy-start | bytes 12292
  15.2 66.4 %all-to-all-start = ((s32[32,1,8]{2,1,0:T(1,128)}), s32[32,1,8]{2,1,0:T(1,128)S(1)}, u32[]{:S(2)}, u32[]{:S(2)}) async-start(s32[32,1,8]{2,1,0:T(1,128)} %copy.18), calls=%async_computation | async-start | bytes 32768 | tf_op jit(solution)/shard_map/all_to_all | solution.py:58
  81.6 15.1 %all-to-all-start.1 = ((bf16[32,8,4,128]{3,2,1,0:T(4,128)(2,1)}), bf16[32,8,4,128]{3,2,1,0:T(4,128)(2,1)S(1)}, u32[]{:S(2)}, u32[]{:S(2)}) async-start(bf16[32,8,4,128]{3,2,1,0:T(4,128)(2,1)} %scatter_fusion.1), calls=%async_computation.1 | async-start | bytes 524288 | tf_op jit(solution)/shard_map/all_to_all | solution.py:73
  86.1 172.8 %all-reduce.6.cloned.1.call-start = ((), (), s32[]{:S(2)}) async-start(), calls=%async_computation.5 | async-start | bytes 4194304
  198.5 1.3 copy-start.1
  199.9 358.0 %all-reduce.8.cloned.1.call-start = ((), (), s32[]{:S(2)}) async-start(), calls=%async_computation.6 | async-start | bytes 4194304
  199.9 4.4 collective-permute-start.1
  201.2 3.9 collective-permute-start
  375.1 259.2 %copy-start.2 = (f32[128,4,128]{2,1,0:T(4,128)}, f32[128,4,128]{2,1,0:T(4,128)S(1)}, u32[]{:S(2)}) copy-start(f32[128,4,128]{2,1,0:T(4,128)S(1)} %get-tuple-element.20) | copy-start | bytes 786436
  497.4 1.3 copy-start
  498.8 4.3 collective-permute-start.3
  500.1 3.9 collective-permute-start.2
Sparse Core Ops, SparseCore 0:
  200.0 58.9 all-reduce.5
  498.8 58.9 all-reduce.7
where the time goes:
time: 652 us; the launch traced here: 642 us
  blocking collectives  243 us (37%)
  other arithmetic  170 us (26%)
  waiting for transfers between devices  93.6 us (14%)
  local copies, waits for them, and re-layouts  63.2 us (10%)
  matrix products  35.8 us (5%)
  starting transfers between devices  20.5 us (3%)
  between operations  15.1 us (2%)
    scatter-add x2, other arithmetic, apply_clustered(): partial_value = jnp.zeros((local_blocks * column_count, sides, width), jn...  133 us
    unnamed x4, waiting for transfers between devices  84.2 us
    psum x1, blocking collectives, body(): lax.psum(local_inner(right_side, right_side), ('row', 'col')) / panels  40.5 us
    psum x1, blocking collectives, body(): lax.psum(local_inner(remainder, remainder), ('row', 'col')) / panels  40 us
    psum x1, blocking collectives, body(): lax.psum(local_inner(first, image_one), ('row', 'col')) / panels  39 us
    psum x1, blocking collectives, body(): lax.psum((local_inner(first, image_two), local_inner(second_basis, image_...  39 us
    all_to_all x2, blocking collectives, relay_out(): lax.all_to_all(outgoing, ('row', 'col'), split_axis=0, concat_axis=0, til...  38.4 us
    all_gather x2, blocking collectives, apply_clustered(): gathered = lax.all_gather(clustered, 'row', axis=0, tiled=True)  31.8 us
  transfers between devices with their start and end apart: 8, of which 5 were waited for; matrix products, arithmetic and copies ran while one was open for 7% of the time, Pallas kernels for 0%

commit v1 on v0

--- a/solution.py
+++ b/solution.py
@@ -90,7 +90,14 @@
         )
         image_sum = 0.5 * clustered.astype(jnp.float32)
         image_sum = image_sum.at[near_rows].add(near_out)
-        gathered = lax.all_gather(clustered, "row", axis=0, tiled=True)
+        ring = [clustered]
+        for hop in range(3):
+            ring.append(lax.ppermute(ring[-1], "row", [(dev, (dev + 1) % 4) for dev in range(4)]))
+        gathered = jnp.roll(
+            jnp.concatenate(ring[::-1], axis=0),
+            (lax.axis_index("row") + 1) * ring[0].shape[0],
+            axis=0,
+        )
         coefficients = jnp.einsum(
             "etp,eqp->etq", far_right, gathered[far_columns], preferred_element_type=jnp.float32
         )

time: 652 us -> 687 us (1.054)
  waiting for transfers between devices: 93.6 us -> 132 us
  blocking collectives: 243 us -> 211 us
  other arithmetic: 170 us -> 193 us
    ppermute x0 -> x6, waiting for transfers between devices: none -> 38.1 us  [apply_clustered(): lax.ppermute(ring[-1], 'row', [(dev, (dev + 1) % 4) for dev in range(4)])]
    all_gather x2 -> x0, blocking collectives: 31.8 us -> none  [apply_clustered(): gathered = lax.all_gather(clustered, 'row', axis=0, tiled=True)]
    concatenate x0 -> x2, other arithmetic: none -> 23.4 us  [apply_clustered(): jnp.roll(jnp.concatenate(ring[::-1], axis=0), (lax.axis_index('row') + 1)...]
  transfers between devices with their start and end apart: 8 -> 14, of which waited for: 5 -> 11; matrix products, arithmetic and copies ran while one was open for 7% -> 6% of each run, Pallas kernels for 0% -> 0%
where the time goes in v1:
time: 687 us; the launch traced here: 674 us
  blocking collectives  211 us (31%)
  other arithmetic  193 us (28%)
  waiting for transfers between devices  132 us (19%)
  local copies, waits for them, and re-layouts  63.3 us (9%)
  matrix products  35.7 us (5%)
  starting transfers between devices  23 us (3%)
  between operations  15.4 us (2%)
    scatter-add x2, other arithmetic, apply_clustered(): partial_value = jnp.zeros((local_blocks * column_count, sides, width), jn...  133 us
    unnamed x4, waiting for transfers between devices  83.4 us
    psum x1, blocking collectives, body(): lax.psum(local_inner(right_side, right_side), ('row', 'col')) / panels  40.5 us
    psum x1, blocking collectives, body(): lax.psum(local_inner(remainder, remainder), ('row', 'col')) / panels  40 us
    psum x1, blocking collectives, body(): lax.psum((local_inner(first, image_two), local_inner(second_basis, image_...  39 us
    psum x1, blocking collectives, body(): lax.psum(local_inner(first, image_one), ('row', 'col')) / panels  39 us
    all_to_all x2, blocking collectives, relay_out(): lax.all_to_all(outgoing, ('row', 'col'), split_axis=0, concat_axis=0, til...  38.4 us
    ppermute x6, waiting for transfers between devices, apply_clustered(): lax.ppermute(ring[-1], 'row', [(dev, (dev + 1) % 4) for dev in range(4)])  38.1 us
  transfers between devices with their start and end apart: 14, of which 11 were waited for; matrix products, arithmetic and copies ran while one was open for 6% of the time, Pallas kernels for 0%

profile of v1, /device:TPU:0, one launch (start us, length us, event | category | flops | bytes accessed | tf_op | source)
XLA Modules:
  0.0 674.2 jit_solution(13600605513830649070)
XLA Ops:
  16.4 7.3 %all-to-all-start = ((s32[32,1,8]{2,1,0:T(1,128)}), s32[32,1,8]{2,1,0:T(1,128)S(1)}, u32[]{:S(2)}, u32[]{:S(2)}) async-start(s32[32,1,8]{2,1,0:T(1,128)} %copy.18), calls=%async_computation | async-start | bytes 32768 | tf_op jit(solution)/shard_map/all_to_all | solution.py:58
  23.7 40.5 %psum.35 = f32[4]{0:T(128)S(1)} all-reduce(f32[4]{0:T(128)S(1)} %multiply_reduce_fusion.4), channel_id=1, replica_groups=mesh['row'=4,'col'=8] {'row','col'}, use_global_device_ids=true, to_apply=%region_3.4 | all-reduce | flops 4 | bytes 32 | tf_op jit(solution)/shard_map/psum | solution.py:125
  66.1 14.8 %scatter_fusion.1 = bf16[32,8,4,128]{3,2,1,0:T(4,128)(2,1)} fusion(bf16[32,8,4,128]{3,2,1,0:T(4,128)(2,1)} %broadcast.147.clone, s32[128]{0:T(128)S(1)} %get-tuple-element.29, bf16[128,4,128]{2,1,0:T(4,128)(2,1)S(1)} %get-tuple-element.22), kind=kCustom, calls=%fused_computation.9 | custom fusion | bytes 394240 | tf_op jit(solution)/shard_map/scatter | solution.py:71
  87.0 9.0 %all-to-all-done.1 = bf16[32,8,4,128]{3,2,1,0:T(4,128)(2,1)S(1)} async-done(((bf16[32,8,4,128]{3,2,1,0:T(4,128)(2,1)}), bf16[32,8,4,128]{3,2,1,0:T(4,128)(2,1)S(1)}, u32[]{:S(2)}, u32[]{:S(2)}) %all-to-all-start.1) | async-done | bytes 262176 | tf_op jit(solution)/shard_map/all_to_all | solution.py:73
  96.0 7.3 %scatter_fusion.2 = bf16[128,4,128]{2,1,0:T(4,128)(2,1)S(1)} fusion(bf16[128,4,128]{2,1,0:T(4,128)(2,1)S(1)} %broadcast.140.clone, s32[256]{0:T(256)S(1)} %bitcast.57, bf16[256,4,128]{2,1,0:T(4,128)(2,1)S(1)} %bitcast.55), kind=kCustom, calls=%fused_computation.10 | custom fusion | bytes 787456 | tf_op jit(solution)/shard_map/scatter | solution.py:78
  124.2 11.7 %fusion.14 = bf16[512,4,128]{2,1,0:T(4,128)(2,1)S(1)} fusion(s32[]{:T(128)S(6)} %select_n.93, bf16[128,4,128]{2,1,0:T(4,128)(2,1)S(1)} %collective-permute-done.2, bf16[128,4,128]{2,1,0:T(4,128)(2,1)S(1)} %collective-permute-done.1, bf16[128,4,128]{2,1,0:T(4,128)(2,1)S(1)} %collective-permute-done, bf16[128,4,128]{2,1,0:T(4,128)(2,1)S(1)} %scatter_fusion.2), kind=kLoop, calls=%fused_computation.49 | loop fusion | flops 1835008 | bytes 1048580 | tf_op jit(solution)/shard_map/jit(_roll_dynamic)/concatenate | solution.py:96
  139.5 8.3 %fusion = f32[1024,4,128]{2,1,0:T(4,128)} fusion(bf16[1024,16,128]{2,1,0:T(8,128)(2,1)} %param.20, bf16[1024,4,128]{2,1,0:T(4,128)(2,1)S(1)} %gather_fusion, bf16[1024,16,128]{2,1,0:T(8,128)(2,1)} %param.21, f32[1024,16]{1,0:T(8,128)S(1)} %fusion.18), kind=kOutput, calls=%fused_computation.19 | convolution fusion | flops 33685504 | bytes 11599872 | tf_op jit(solution)/shard_map/etq,etk->eqk/dot_general | solution.py:105
  148.1 66.4 %scatter_fusion.3 = f32[1024,4,128]{2,1,0:T(4,128)S(1)} fusion(f32[1024,4,128]{2,1,0:T(4,128)S(1)} %broadcast.151.clone, s32[1024]{0:T(1024)S(1)} %compare_select_fusion.1, f32[1024,4,128]{2,1,0:T(4,128)} %fusion), kind=kCustom, calls=%fused_computation.11 | custom fusion | flops 524288 | bytes 6295552 | tf_op jit(solution)/shard_map/scatter-add | solution.py:111
  223.3 9.6 %fusion.34 = f32[384,4,128]{2,1,0:T(4,128)S(1)} fusion(bf16[384,4,128]{2,1,0:T(4,128)(2,1)S(1)} %gather_fusion.1, bf16[384,128,128]{2,1,0:T(8,128)(2,1)} %param.16), kind=kOutput, calls=%fused_computation.108 | convolution fusion | flops 50331648 | bytes 13762560 | tf_op jit(solution)/shard_map/ekp,eqp->eqk/dot_general | solution.py:88
  232.8 41.7 %all-reduce.6.cloned.1.call-done = f32[1024,4,128]{2,1,0:T(4,128)} async-done(((f32[1024,4,128]{2,1,0:T(4,128)}), f32[1024,4,128]{2,1,0:T(4,128)}) %all-reduce.6.cloned.1.call-update) | async-done | bytes 2097168
  275.5 14.2 %scatter_fusion.4 = f32[128,4,128]{2,1,0:T(4,128)S(1)} fusion(f32[128,4,128]{2,1,0:T(4,128)S(1)} %dynamic-slice_add_fusion.1, s32[384]{0:T(512)S(1)} %compare_select_fusion.5, f32[384,4,128]{2,1,0:T(4,128)S(1)} %fusion.34), kind=kCustom, calls=%fused_computation.12 | custom fusion | flops 196608 | bytes 2360832 | tf_op jit(solution)/shard_map/scatter-add | solution.py:92
  290.8 19.2 %all_to_all.29 = f32[32,8,4,128]{3,2,1,0:T(4,128)S(1)} all-to-all(f32[32,8,4,128]{3,2,1,0:T(4,128)S(1)} %bitcast.54), channel_id=1, replica_groups=mesh['row'=4,'col'=8] {'row','col'}, dimensions={0} | all-to-all | bytes 1048576 | tf_op jit(solution)/shard_map/all_to_all | solution.py:83
  311.2 39.0 %psum.36 = f32[4]{0:T(128)S(1)} all-reduce(f32[4]{0:T(128)S(1)} %multiply_reduce_fusion.3), channel_id=1, replica_groups=mesh['row'=4,'col'=8] {'row','col'}, use_global_device_ids=true, to_apply=%region_10.12 | all-reduce | flops 4 | bytes 32 | tf_op jit(solution)/shard_map/psum | solution.py:129
  350.5 40.0 %psum.37 = f32[4]{0:T(128)S(1)} all-reduce(f32[4]{0:T(128)S(1)} %multiply_reduce_fusion.2), channel_id=1, replica_groups=mesh['row'=4,'col'=8] {'row','col'}, use_global_device_ids=true, to_apply=%region_12.14 | all-reduce | flops 4 | bytes 32 | tf_op jit(solution)/shard_map/psum | solution.py:132
  396.5 14.6 %all_to_all.30 = bf16[32,8,4,128]{3,2,1,0:T(4,128)(2,1)S(1)} all-to-all(bf16[32,8,4,128]{3,2,1,0:T(4,128)(2,1)S(1)} %scatter_fusion.5), channel_id=1, replica_groups=mesh['row'=4,'col'=8] {'row','col'}, dimensions={0} | all-to-all | bytes 524288 | tf_op jit(solution)/shard_map/all_to_all | solution.py:73
  411.1 7.3 %scatter_fusion.6 = bf16[128,4,128]{2,1,0:T(4,128)(2,1)S(1)} fusion(bf16[128,4,128]{2,1,0:T(4,128)(2,1)S(1)} %broadcast.140, s32[256]{0:T(256)S(1)} %bitcast.58, bf16[256,4,128]{2,1,0:T(4,128)(2,1)S(1)} %bitcast.56), kind=kCustom, calls=%fused_computation.14 | custom fusion | bytes 787456 | tf_op jit(solution)/shard_map/scatter | solution.py:78
  439.5 11.7 %fusion.7 = bf16[512,4,128]{2,1,0:T(4,128)(2,1)S(1)} fusion(s32[]{:T(128)S(6)} %select_n.93, bf16[128,4,128]{2,1,0:T(4,128)(2,1)S(1)} %collective-permute-done.7, bf16[128,4,128]{2,1,0:T(4,128)(2,1)S(1)} %collective-permute-done.6, bf16[128,4,128]{2,1,0:T(4,128)(2,1)S(1)} %collective-permute-done.5, bf16[128,4,128]{2,1,0:T(4,128)(2,1)S(1)} %scatter_fusion.6), kind=kLoop, calls=%fused_computation.42 | loop fusion | flops 1835008 | bytes 1048580 | tf_op jit(solution)/shard_map/jit(_roll_dynamic)/concatenate | solution.py:96
  454.8 8.3 %fusion.1 = f32[1024,4,128]{2,1,0:T(4,128)} fusion(bf16[1024,16,128]{2,1,0:T(8,128)(2,1)} %param.20, bf16[1024,4,128]{2,1,0:T(4,128)(2,1)S(1)} %gather_fusion.4, bf16[1024,16,128]{2,1,0:T(8,128)(2,1)} %param.21, f32[1024,16]{1,0:T(8,128)S(1)} %fusion.18), kind=kOutput, calls=%fused_computation.20 | convolution fusion | flops 33685504 | bytes 11599872 | tf_op jit(solution)/shard_map/etq,etk->eqk/dot_general | solution.py:105
  463.4 66.4 %scatter_fusion.7 = f32[1024,4,128]{2,1,0:T(4,128)S(1)} fusion(f32[1024,4,128]{2,1,0:T(4,128)S(1)} %broadcast.151, s32[1024]{0:T(1024)S(1)} %compare_select_fusion.1, f32[1024,4,128]{2,1,0:T(4,128)} %fusion.1), kind=kCustom, calls=%fused_computation.15 | custom fusion | flops 524288 | bytes 6295552 | tf_op jit(solution)/shard_map/scatter-add | solution.py:111
  538.5 9.6 %fusion.35 = f32[384,4,128]{2,1,0:T(4,128)S(1)} fusion(bf16[384,4,128]{2,1,0:T(4,128)(2,1)S(1)} %gather_fusion.5, bf16[384,128,128]{2,1,0:T(8,128)(2,1)} %param.16), kind=kOutput, calls=%fused_computation.109 | convolution fusion | flops 50331648 | bytes 13762560 | tf_op jit(solution)/shard_map/ekp,eqp->eqk/dot_general | solution.py:88
  548.1 41.8 %all-reduce.8.cloned.1.call-done = f32[1024,4,128]{2,1,0:T(4,128)} async-done(((f32[1024,4,128]{2,1,0:T(4,128)}), f32[1024,4,128]{2,1,0:T(4,128)}) %all-reduce.8.cloned.1.call-update) | async-done | bytes 2097168
  590.9 14.2 %scatter_fusion.8 = f32[128,4,128]{2,1,0:T(4,128)S(1)} fusion(f32[128,4,128]{2,1,0:T(4,128)S(1)} %dynamic-slice_add_fusion, s32[384]{0:T(512)S(1)} %compare_select_fusion.5, f32[384,4,128]{2,1,0:T(4,128)S(1)} %fusion.35), kind=kCustom, calls=%fused_computation.16 | custom fusion | flops 196608 | bytes 2360832 | tf_op jit(solution)/shard_map/scatter-add | solution.py:92
  606.1 19.2 %all_to_all.31 = f32[32,8,4,128]{3,2,1,0:T(4,128)S(1)} all-to-all(f32[32,8,4,128]{3,2,1,0:T(4,128)S(1)} %bitcast.53), channel_id=1, replica_groups=mesh['row'=4,'col'=8] {'row','col'}, dimensions={0} | all-to-all | bytes 1048576 | tf_op jit(solution)/shard_map/all_to_all | solution.py:83
  626.6 39.0 %all-reduce.2 = (f32[4]{0:T(128)S(1)}, f32[4]{0:T(128)S(1)}) all-reduce(f32[4]{0:T(128)S(1)} %get-tuple-element.17, f32[4]{0:T(128)S(1)} %get-tuple-element.16), channel_id=1, replica_groups=mesh['row'=4,'col'=8] {'row','col'}, use_global_device_ids=true, to_apply=%region_21.23 | all-reduce | flops 8 | bytes 64 | tf_op jit(solution)/shard_map/psum | solution.py:136
  (96 shorter events, 97.8 us)
Async XLA Ops:
  7.2 78.3 %copy-start.4 = (s32[1024]{0:T(1024)S(1)}, s32[1024]{0:T(1024)}, u32[]{:S(2)}) copy-start(s32[1024]{0:T(1024)} %param.17) | copy-start | bytes 12292
  7.2 78.3 %copy-start.3 = (s32[1024]{0:T(1024)S(1)}, s32[1024]{0:T(1024)}, u32[]{:S(2)}) copy-start(s32[1024]{0:T(1024)} %param.19) | copy-start | bytes 12292
  14.5 89.8 %copy-start.5 = (s32[1024]{0:T(1024)S(1)}, s32[1024]{0:T(1024)}, u32[]{:S(2)}) copy-start(s32[1024]{0:T(1024)} %param.18) | copy-start | bytes 12292
  14.5 96.0 %copy-start.6 = (s32[384]{0:T(512)S(1)}, s32[384]{0:T(512)}, u32[]{:S(2)}) copy-start(s32[384]{0:T(512)} %param.14) | copy-start | bytes 4612
  14.5 102.9 %copy-start.7 = (s32[384]{0:T(512)S(1)}, s32[384]{0:T(512)}, u32[]{:S(2)}) copy-start(s32[384]{0:T(512)} %param.15) | copy-start | bytes 4612
  14.5 103.0 %copy-start.8 = (u32[32]{0:T(128)S(1)}, u32[32]{0:T(128)}, u32[]{:S(2)}) copy-start(u32[32]{0:T(128)} %constant.163) | copy-start | bytes 388
  16.4 64.5 %all-to-all-start = ((s32[32,1,8]{2,1,0:T(1,128)}), s32[32,1,8]{2,1,0:T(1,128)S(1)}, u32[]{:S(2)}, u32[]{:S(2)}) async-start(s32[32,1,8]{2,1,0:T(1,128)} %copy.18), calls=%async_computation | async-start | bytes 32768 | tf_op jit(solution)/shard_map/all_to_all | solution.py:58
  80.9 15.1 %all-to-all-start.1 = ((bf16[32,8,4,128]{3,2,1,0:T(4,128)(2,1)}), bf16[32,8,4,128]{3,2,1,0:T(4,128)(2,1)S(1)}, u32[]{:S(2)}, u32[]{:S(2)}) async-start(bf16[32,8,4,128]{3,2,1,0:T(4,128)(2,1)} %scatter_fusion.1), calls=%async_computation.1 | async-start | bytes 524288 | tf_op jit(solution)/shard_map/all_to_all | solution.py:73
  85.4 189.1 %all-reduce.6.cloned.1.call-start = ((), (), s32[]{:S(2)}) async-start(), calls=%async_computation.5 | async-start | bytes 4194304
  103.4 7.2 %collective-permute-start = (bf16[128,4,128]{2,1,0:T(4,128)(2,1)S(1)}, bf16[128,4,128]{2,1,0:T(4,128)(2,1)S(1)}, u32[]{:S(2)}, u32[]{:S(2)}) collective-permute-start(bf16[128,4,128]{2,1,0:T(4,128)(2,1)S(1)} %scatter_fusion.2), channel_id=1, source_target_pairs={{0,8},{8,16},{16,24},{24,0},{1,9},{9,17},{17,25},{25,1},{2,10},{10... | collective-permute-start | bytes 393224 | tf_op jit(solution)/shard_map/ppermute | solution.py:95
  110.5 6.8 %collective-permute-start.1 = (bf16[128,4,128]{2,1,0:T(4,128)(2,1)S(1)}, bf16[128,4,128]{2,1,0:T(4,128)(2,1)S(1)}, u32[]{:S(2)}, u32[]{:S(2)}) collective-permute-start(bf16[128,4,128]{2,1,0:T(4,128)(2,1)S(1)} %collective-permute-done), channel_id=1, source_target_pairs={{0,8},{8,16},{16,24},{24,0},{1,9},{9,17},{17,25},{25,1},{2,10},{10... | collective-permute-start | bytes 393224 | tf_op jit(solution)/shard_map/ppermute | solution.py:95
  117.3 6.9 %collective-permute-start.2 = (bf16[128,4,128]{2,1,0:T(4,128)(2,1)S(1)}, bf16[128,4,128]{2,1,0:T(4,128)(2,1)S(1)}, u32[]{:S(2)}, u32[]{:S(2)}) collective-permute-start(bf16[128,4,128]{2,1,0:T(4,128)(2,1)S(1)} %collective-permute-done.1), channel_id=1, source_target_pairs={{0,8},{8,16},{16,24},{24,0},{1,9},{9,17},{17,25},{25,1},{2,10},{10... | collective-permute-start | bytes 393224 | tf_op jit(solution)/shard_map/ppermute | solution.py:95
  214.5 1.3 copy-start.1
  215.8 374.0 %all-reduce.8.cloned.1.call-start = ((), (), s32[]{:S(2)}) async-start(), calls=%async_computation.6 | async-start | bytes 4194304
  215.9 4.4 collective-permute-start.4
  217.2 3.9 collective-permute-start.3
  390.7 275.6 %copy-start.2 = (f32[128,4,128]{2,1,0:T(4,128)}, f32[128,4,128]{2,1,0:T(4,128)S(1)}, u32[]{:S(2)}) copy-start(f32[128,4,128]{2,1,0:T(4,128)S(1)} %get-tuple-element.21) | copy-start | bytes 786436
  418.5 7.2 %collective-permute-start.5 = (bf16[128,4,128]{2,1,0:T(4,128)(2,1)S(1)}, bf16[128,4,128]{2,1,0:T(4,128)(2,1)S(1)}, u32[]{:S(2)}, u32[]{:S(2)}) collective-permute-start(bf16[128,4,128]{2,1,0:T(4,128)(2,1)S(1)} %scatter_fusion.6), channel_id=1, source_target_pairs={{0,8},{8,16},{16,24},{24,0},{1,9},{9,17},{17,25},{25,1},{2,10},{10... | collective-permute-start | bytes 393224 | tf_op jit(solution)/shard_map/ppermute | solution.py:95
  425.6 6.8 %collective-permute-start.6 = (bf16[128,4,128]{2,1,0:T(4,128)(2,1)S(1)}, bf16[128,4,128]{2,1,0:T(4,128)(2,1)S(1)}, u32[]{:S(2)}, u32[]{:S(2)}) collective-permute-start(bf16[128,4,128]{2,1,0:T(4,128)(2,1)S(1)} %collective-permute-done.5), channel_id=1, source_target_pairs={{0,8},{8,16},{16,24},{24,0},{1,9},{9,17},{17,25},{25,1},{2,10},{10... | collective-permute-start | bytes 393224 | tf_op jit(solution)/shard_map/ppermute | solution.py:95
  432.4 7.1 %collective-permute-start.7 = (bf16[128,4,128]{2,1,0:T(4,128)(2,1)S(1)}, bf16[128,4,128]{2,1,0:T(4,128)(2,1)S(1)}, u32[]{:S(2)}, u32[]{:S(2)}) collective-permute-start(bf16[128,4,128]{2,1,0:T(4,128)(2,1)S(1)} %collective-permute-done.6), channel_id=1, source_target_pairs={{0,8},{8,16},{16,24},{24,0},{1,9},{9,17},{17,25},{25,1},{2,10},{10... | collective-permute-start | bytes 393224 | tf_op jit(solution)/shard_map/ppermute | solution.py:95
  529.8 1.3 copy-start
  531.1 4.3 collective-permute-start.9
  532.4 3.9 collective-permute-start.8
Sparse Core Ops, SparseCore 0:
  215.9 58.5 all-reduce.5
  531.2 58.5 all-reduce.7
